TPU v7x, 32 devices: a whole 2x2x4 slice. The times are simulated.
32 devices in a mesh: tm: 16 (over z, x, core), mp: 2 (over y).
Axes of the slice: x: 2, y: 2, z: 4, core: 2. Of those that a mesh axis runs over, the one named last changes fastest.
Arguments:
- tokens: bfloat16 [4096, 1024], P('tm'), may hold values from -9 to 9
- norm1_gain: float32 [1024], replicated, may hold values from 0.5 to 1.5
- query_weight: bfloat16 [1024, 1024], P(None, 'mp'), may hold values from -1 to 1
- key_weight: bfloat16 [1024, 1024], P(None, 'mp'), may hold values from -1 to 1
- value_weight: bfloat16 [1024, 1024], P(None, 'mp'), may hold values from -0.1875 to 0.1875
- output_weight: bfloat16 [1024, 1024], P('mp'), may hold values from -5 to 5
- pattern: int32 [32, 8], replicated, may hold values from -1 to 31, as said below
- adjacency: int32 [128, 128], replicated, may hold values 0 or 1
- decay_rate: float32 [1024], P('mp'), may hold values from 0.015625 to 0.1
- norm2_gain: float32 [1024], replicated, may hold values from 0.5 to 1.5
- up_weight: bfloat16 [1024, 4096], P(None, 'mp'), may hold values from -0.1875 to 0.1875
- down_weight: bfloat16 [4096, 1024], P('mp'), may hold values from -0.09375 to 0.09375
Outputs:
- layer_out: bfloat16 [4096, 1024], P('tm', 'mp')
Inputs may be any that keep to these rules, and one draw needn't show every extreme that they name: pattern[b, 0] = b and pattern[b, 1] = b - 1. For the rows of the blocks g * 2 to g * 2 + 1, entry 2 + k (k from 0 to 5) is the same in all these rows: -1 where g < 2^k, else one of the blocks (g - 2^k) * 2 to (g - 2^k) * 2 + 1, never the block g * 2 - 1.
All inputs are finite; a program needn't handle non-finite values.
Results may differ from a plain program's by a relative error of at most 0.01.
Values may be sent and summed in bfloat16 or wider, within the bound.
A program may use at most 64 MiB of HBM per device.

v0:
```python
import math

import jax
import jax.numpy as jnp
from jax import lax
from jax.sharding import PartitionSpec as P

HD = 128


def from_behind(value, axis, steps):
    count = lax.axis_size(axis)
    first, last = (max(0, -steps), min(count, count - steps))
    return lax.ppermute(value, axis, [(source, source + steps) for source in range(first, last)])


def rms_norm(rows, gain):
    widened = rows.astype(jnp.float32)
    square = jnp.mean(widened * widened, axis=-1, keepdims=True)
    return (widened * lax.rsqrt(square + 1e-05) * gain).astype(jnp.bfloat16)


def block_partial(queries, key_rows, value_rows, heads):
    head_size = queries.shape[-1] // heads
    query_split = queries.reshape(queries.shape[:-1] + (heads, head_size))
    key_split = key_rows.reshape(key_rows.shape[:-1] + (heads, head_size))
    value_split = value_rows.reshape(value_rows.shape[:-1] + (heads, head_size))
    scores = jnp.einsum(
        "...qhd,...khd->...hqk", query_split, key_split, preferred_element_type=jnp.float32
    ) * (1.0 / math.sqrt(head_size))
    tops = jnp.max(scores, axis=-1)
    probs = jnp.exp(scores - tops[..., None])
    totals = jnp.sum(probs, axis=-1)
    weights = probs.astype(jnp.bfloat16)
    outputs = jnp.einsum(
        "...hqk,...khd->...qhd", weights, value_split, preferred_element_type=jnp.float32
    )
    return (tops, totals, outputs.reshape(outputs.shape[:-2] + (heads * head_size,)))


def merge_partials(tops, totals, outputs, valid, heads):
    flags = valid[..., None, None]
    masked = jnp.where(flags, tops, -jnp.inf)
    largest = jnp.max(masked, axis=-3)
    factor = jnp.where(flags, jnp.exp(jnp.where(flags, tops, 0.0) - largest[..., None, :, :]), 0.0)
    denom = jnp.sum(factor * totals, axis=-3)
    split = outputs.reshape(outputs.shape[:-1] + (heads, -1))
    numer = jnp.sum(jnp.swapaxes(factor, -1, -2)[..., None] * split, axis=-4)
    result = numer / jnp.swapaxes(denom, -1, -2)[..., None]
    return result.reshape(result.shape[:-2] + (-1,)).astype(jnp.bfloat16)


def running(frames, retain, inject):
    driven = frames.astype(jnp.float32) * inject
    factors = jnp.broadcast_to(retain, driven.shape)

    def join(earlier, later):
        return (earlier[0] * later[0], later[0] * earlier[1] + later[1])

    return lax.associative_scan(join, (factors, driven), axis=0)[1]


def per_device(
    tokens,
    norm1_gain,
    query_weight,
    key_weight,
    value_weight,
    output_weight,
    pattern,
    adjacency,
    decay_rate,
    norm2_gain,
    up_weight,
    down_weight,
):
    groups = lax.axis_size("tm")
    position = lax.axis_index("tm")
    width = query_weight.shape[1]
    heads = width // HD
    sites = adjacency.shape[0]
    steps = tokens.shape[0] // sites
    normed = rms_norm(tokens, norm1_gain)
    queries = (
        jnp.dot(normed, query_weight, preferred_element_type=jnp.float32)
        .astype(jnp.bfloat16)
        .reshape(steps, sites, width)
    )
    key_rows = jnp.dot(normed, key_weight, preferred_element_type=jnp.float32).astype(jnp.bfloat16)
    value_rows = jnp.dot(normed, value_weight, preferred_element_type=jnp.float32).astype(
        jnp.bfloat16
    )
    key_blocks = key_rows.reshape(steps, sites, width)
    value_blocks = value_rows.reshape(steps, sites, width)
    own_entries = lax.dynamic_slice_in_dim(pattern, position * steps, steps, 0)
    remote = own_entries[:, 2:]
    far_count = remote.shape[1]
    key_last, value_last = from_behind((key_blocks[steps - 1], value_blocks[steps - 1]), "tm", 1)
    prior_keys = jnp.concatenate([key_last[None], key_blocks[:-1]], axis=0)
    prior_values = jnp.concatenate([value_last[None], value_blocks[:-1]], axis=0)
    self_part = block_partial(queries, key_blocks, value_blocks, heads)
    prior_part = block_partial(queries, prior_keys, prior_values, heads)
    spread_queries = jnp.broadcast_to(queries[:, None], (steps, far_count, sites, width))
    wanted = pattern[:, 2:].reshape(groups, -1)
    local_pick = wanted - position * steps
    hits = (wanted >= 0) & (local_pick >= 0) & (local_pick < steps)
    selector = jnp.any(
        (local_pick[:, :, None] == jnp.arange(steps, dtype=jnp.int32)[None, None, :])
        & hits[:, :, None],
        axis=1,
    ).astype(jnp.bfloat16)
    send_keys = jnp.einsum(
        "gs,sbf->gbf", selector, key_blocks, preferred_element_type=jnp.float32
    ).astype(jnp.bfloat16)
    send_values = jnp.einsum(
        "gs,sbf->gbf", selector, value_blocks, preferred_element_type=jnp.float32
    ).astype(jnp.bfloat16)
    got_keys, got_values = (
        lax.all_to_all(send_keys, "tm", split_axis=0, concat_axis=0, tiled=True),
        lax.all_to_all(send_values, "tm", split_axis=0, concat_axis=0, tiled=True),
    )
    source = jnp.maximum(remote, 0) // steps
    far_part = block_partial(spread_queries, got_keys[source], got_values[source], heads)
    tops = jnp.concatenate([self_part[0][:, None], prior_part[0][:, None], far_part[0]], axis=1)
    totals = jnp.concatenate([self_part[1][:, None], prior_part[1][:, None], far_part[1]], axis=1)
    outputs = jnp.concatenate([self_part[2][:, None], prior_part[2][:, None], far_part[2]], axis=1)
    block_ids = position * steps + jnp.arange(steps, dtype=jnp.int32)
    valid = jnp.concatenate(
        [jnp.ones((steps, 1), bool), (block_ids > 0)[:, None], remote >= 0], axis=1
    )
    attended = merge_partials(tops, totals, outputs, valid, heads).reshape(steps * sites, width)
    projected = lax.psum_scatter(
        jnp.dot(attended, output_weight, preferred_element_type=jnp.float32),
        "mp",
        scatter_dimension=1,
        tiled=True,
    )
    columns = projected.shape[1]
    own_tokens = lax.dynamic_slice_in_dim(tokens, lax.axis_index("mp") * columns, columns, 1)
    first = (own_tokens.astype(jnp.float32) + projected).astype(jnp.bfloat16)
    links = jnp.maximum(adjacency, jnp.eye(sites, dtype=jnp.int32))
    degree = jnp.sum(links, axis=1).astype(jnp.float32)
    grid = first.reshape(steps, sites, columns)
    mixed = (
        jnp.einsum(
            "st,btc->bsc", links.astype(jnp.bfloat16), grid, preferred_element_type=jnp.float32
        )
        / degree[None, :, None]
    ).astype(jnp.bfloat16)
    retain = jnp.exp(-decay_rate)
    inject = jnp.sqrt(1.0 - retain * retain)
    by_site = lax.all_to_all(mixed, "tm", split_axis=1, concat_axis=0, tiled=True)
    states = running(by_site, retain, inject).astype(jnp.bfloat16)
    smoothed = lax.all_to_all(states, "tm", split_axis=0, concat_axis=1, tiled=True)
    second = (
        first.astype(jnp.float32) + smoothed.reshape(steps * sites, columns).astype(jnp.float32)
    ).astype(jnp.bfloat16)
    whole = lax.all_gather(second, "mp", axis=1, tiled=True)
    normed_late = rms_norm(whole, norm2_gain)
    hidden = jax.nn.gelu(
        jnp.dot(normed_late, up_weight, preferred_element_type=jnp.float32), approximate=True
    ).astype(jnp.bfloat16)
    summed = lax.psum_scatter(
        jnp.dot(hidden, down_weight, preferred_element_type=jnp.float32),
        "mp",
        scatter_dimension=1,
        tiled=True,
    )
    return (second.astype(jnp.float32) + summed).astype(jnp.bfloat16)


def solution(mesh):
    placed = (
        P("tm", None),
        P(),
        P(None, "mp"),
        P(None, "mp"),
        P(None, "mp"),
        P("mp", None),
        P(),
        P(),
        P("mp"),
        P(),
        P(None, "mp"),
        P("mp", None),
    )
    return jax.shard_map(
        per_device, mesh=mesh, in_specs=placed, out_specs=P("tm", "mp"), check_vma=False
    )
```

profile of v0, /device:TPU:24, one launch (start us, length us, event | category | flops | bytes accessed | tf_op | source)
XLA Modules:
  0.0 241.7 jit_solution(6739945608081619143)
XLA Ops:
  6.5 1.3 fusion.16
  7.9 0.7 slice_compare_fusion
  9.7 1.9 convolution_convert_fusion.2
  11.6 0.8 convolution_convert_fusion
  12.4 2.5 %copy.148 = bf16[16,128,512]{2,1,0:T(8,128)(2,1)} copy(bf16[16,128,512]{2,0,1:T(8,128)(2,1)S(1)} %convolution_convert_fusion) | data formatting | bytes 4194304 | tf_op jit(solution)/shard_map/convert_element_type | solution.py:117
  15.0 6.2 %all-to-all-start.1 = ((bf16[16,128,512]{2,1,0:T(8,128)(2,1)}), bf16[16,128,512]{2,1,0:T(8,128)(2,1)S(1)}, u32[]{:S(2)}, u32[]{:S(2)}) async-start(bf16[16,128,512]{2,1,0:T(8,128)(2,1)} %copy.148), calls=%async_computation.1 | async-start | bytes 4194304 | tf_op jit(solution)/shard_map/all_to_all | solution.py:120
  21.1 1.9 convolution_convert_fusion.3
  23.7 0.8 convolution_convert_fusion.1
  24.5 2.5 %copy.138 = bf16[16,128,512]{2,1,0:T(8,128)(2,1)} copy(bf16[16,128,512]{2,0,1:T(8,128)(2,1)S(1)} %convolution_convert_fusion.1) | data formatting | bytes 4194304 | tf_op jit(solution)/shard_map/convert_element_type | solution.py:114
  27.0 37.6 %all-to-all-done.1 = bf16[16,128,512]{2,1,0:T(8,128)(2,1)S(1)} async-done(((bf16[16,128,512]{2,1,0:T(8,128)(2,1)}), bf16[16,128,512]{2,1,0:T(8,128)(2,1)S(1)}, u32[]{:S(2)}, u32[]{:S(2)}) %all-to-all-start.1) | async-done | bytes 2097184 | tf_op jit(solution)/shard_map/all_to_all | solution.py:120
  64.6 8.8 %all-to-all-start = ((bf16[16,128,512]{2,1,0:T(8,128)(2,1)}), bf16[16,128,512]{2,1,0:T(8,128)(2,1)}, u32[]{:S(2)}, u32[]{:S(2)}) async-start(bf16[16,128,512]{2,1,0:T(8,128)(2,1)} %copy.138), calls=%async_computation | async-start | bytes 4194304 | tf_op jit(solution)/shard_map/all_to_all | solution.py:119
  73.5 1.7 fusion.94
  75.2 2.0 collective-permute-start
  77.3 0.7 fusion.93
  78.0 3.5 %collective-permute-start.1 = (bf16[128,512]{1,0:T(8,128)(2,1)}, bf16[128,512]{1,0:T(8,128)(2,1)}, u32[]{:S(2)}, u32[]{:S(2)}) collective-permute-start(bf16[128,512]{1,0:T(8,128)(2,1)} %get-tuple-element.5), channel_id=1, source_target_pairs={{0,2},{2,4},{4,6},{6,8},{8,10},{10,12},{12,14},{14,16},{16,18},{18... | collective-permute-start | bytes 393224 | tf_op jit(solution)/shard_map/ppermute | solution.py:14
  81.5 1.7 reshape_reshape.11
  83.2 0.8 reshape_reshape.12
  84.2 2.6 %convolution_convert_fusion.4 = bf16[256,512]{1,0:T(8,128)(2,1)} fusion(bf16[1024,512]{1,0:T(8,128)(2,1)} %param.14, bf16[256,1024]{1,0:T(8,128)(2,1)} %param.12, f32[1024]{0:T(1024)S(1)} %copy-done.11, f32[256]{0:T(256)S(1)} %add_rsqrt_fusion.1), kind=kOutput, calls=%fused_computation.34 | convolution fusion | flops 269615104 | bytes 1840128 | tf_op jit(solution)/shard_map/dot_general | solution.py:85
  86.8 1.0 reshape_reshape.10
  87.8 0.7 copy.129
  88.6 0.9 concatenate.47
  90.2 1.0 copy.165
  91.9 1.3 fusion.97
  93.2 2.0 convolution_bitcast_fusion.2
  95.3 4.8 %collective-permute-done = bf16[128,512]{1,0:T(8,128)(2,1)} collective-permute-done((bf16[128,512]{1,0:T(8,128)(2,1)}, bf16[128,512]{1,0:T(8,128)(2,1)}, u32[]{:S(2)}, u32[]{:S(2)}) %collective-permute-start) | collective-permute-done | bytes 131104 | tf_op jit(solution)/shard_map/ppermute | solution.py:14
  100.1 1.6 concatenate.46
  101.7 1.6 copy.131
  103.3 1.7 copy.164
  104.9 1.3 fusion.96
  106.3 2.0 convolution_bitcast_fusion.1
  108.3 1.9 gather_fusion.1
  110.2 2.6 %copy.149 = bf16[12,128,512]{1,2,0:T(8,128)(2,1)} copy(bf16[12,128,512]{2,1,0:T(8,128)(2,1)} %gather_fusion.1) | data formatting | bytes 3145728 | tf_op jit(solution)/shard_map/gather | solution.py:123
  112.8 4.4 %all-to-all-done = bf16[16,128,512]{2,1,0:T(8,128)(2,1)} async-done(((bf16[16,128,512]{2,1,0:T(8,128)(2,1)}), bf16[16,128,512]{2,1,0:T(8,128)(2,1)}, u32[]{:S(2)}, u32[]{:S(2)}) %all-to-all-start) | async-done | bytes 2097184 | tf_op jit(solution)/shard_map/all_to_all | solution.py:119
  117.1 3.4 %gather_fusion = bf16[12,128,512]{2,1,0:T(8,128)(2,1)} fusion(bf16[16,128,512]{2,1,0:T(8,128)(2,1)} %all-to-all-done, s32[1024]{0:T(1024)S(1)} %pad_clamp_fusion), kind=kCustom, calls=%fused_computation | custom fusion | bytes 3145776 | tf_op jit(solution)/shard_map/gather | solution.py:123
  120.6 1.9 copy.140
  122.5 1.3 multiply_reduce_fusion
  124.5 0.7 copy-done.1
  127.2 1.4 fusion.47
  128.8 37.7 %reduce-scatter.3.cloned.1.call-done = f32[256,512]{1,0:T(8,128)} async-done(((f32[256,1024]{1,0:T(8,128)}), f32[256,512]{1,0:T(8,128)}) %reduce-scatter.3.cloned.1.call-update) | async-done | bytes 524304 | tf_op jit(solution)/shard_map/reduce_scatter | solution.py:132
  166.5 1.1 add_convert_fusion.2
  167.9 0.9 copy.155
  168.7 6.0 %all-to-all-start.2 = ((bf16[2,128,512]{2,0,1:T(2,128)(2,1)}), bf16[2,128,512]{2,0,1:T(2,128)(2,1)S(1)}, u32[]{:S(2)}, u32[]{:S(2)}) async-start(bf16[2,128,512]{2,0,1:T(2,128)(2,1)} %copy.155), calls=%async_computation.3 | async-start | bytes 524288 | tf_op jit(solution)/shard_map/all_to_all | solution.py:152
  174.8 7.2 %all-to-all-done.2 = bf16[2,128,512]{2,0,1:T(2,128)(2,1)S(1)} async-done(((bf16[2,128,512]{2,0,1:T(2,128)(2,1)}), bf16[2,128,512]{2,0,1:T(2,128)(2,1)S(1)}, u32[]{:S(2)}, u32[]{:S(2)}) %all-to-all-start.2) | async-done | bytes 262176 | tf_op jit(solution)/shard_map/all_to_all | solution.py:152
  183.4 12.8 %all_to_all.28 = bf16[32,8,512]{2,1,0:T(8,128)(2,1)S(1)} all-to-all(bf16[32,8,512]{2,1,0:T(8,128)(2,1)S(1)} %add_convert_fusion.1), channel_id=1, replica_groups=mesh['tm'=16,'mp'=2] {'tm'}, dimensions={0} | all-to-all | bytes 524288 | tf_op jit(solution)/shard_map/all_to_all | solution.py:154
  196.4 9.3 %all_gather.3 = bf16[256,1024]{1,0:T(8,128)(2,1)S(1)} all-gather(bf16[256,512]{1,0:T(8,128)(2,1)S(1)} %fusion.36), channel_id=1, replica_groups=mesh['tm'=16,'mp'=2] {'mp'}, dimensions={1}, use_global_device_ids=true | all-gather | bytes 786432 | tf_op jit(solution)/shard_map/all_gather | solution.py:158
  205.9 7.1 %fusion.22 = f32[256,1024]{1,0:T(8,128)} fusion(bf16[2048,1024]{1,0:T(8,128)(2,1)} %param.23, bf16[1024,2048]{1,0:T(8,128)(2,1)} %param.22, bf16[256,1024]{1,0:T(8,128)(2,1)S(1)} %all_gather.3, f32[1024]{0:T(1024)S(1)} %copy-done.12, f32[256]{0:T(256)S(1)} %add_rsqrt_fusion), kind=kOutput, calls=%fused_computation.42 | convolution fusion | flops 2153250816 | bytes 9966592 | tf_op jit(solution)/shard_map/dot_general | solution.py:164
  213.1 20.0 %reduce-scatter.5.cloned.1.call-done = f32[256,512]{1,0:T(8,128)} async-done(((f32[256,1024]{1,0:T(8,128)}), f32[256,512]{1,0:T(8,128)}) %reduce-scatter.5.cloned.1.call-update) | async-done | bytes 524304 | tf_op jit(solution)/shard_map/reduce_scatter | solution.py:163
  233.0 1.8 add_convert_fusion
  (99 shorter events, 8.3 us)
Async XLA Ops:
  6.5 120.7 %copy-start = (bf16[512,1024]{1,0:T(8,128)(2,1)S(1)}, bf16[512,1024]{1,0:T(8,128)(2,1)}, u32[]{:S(2)}) copy-start(bf16[512,1024]{1,0:T(8,128)(2,1)} %param.17) | copy-start | bytes 3145732
  15.0 6.2 %copy-start.11 = (f32[1024]{0:T(1024)S(1)}, f32[1024]{0:T(1024)}, u32[]{:S(2)}) copy-start(f32[1024]{0:T(1024)} %param.13) | copy-start | bytes 12292
  15.0 49.7 %all-to-all-start.1 = ((bf16[16,128,512]{2,1,0:T(8,128)(2,1)}), bf16[16,128,512]{2,1,0:T(8,128)(2,1)S(1)}, u32[]{:S(2)}, u32[]{:S(2)}) async-start(bf16[16,128,512]{2,1,0:T(8,128)(2,1)} %copy.148), calls=%async_computation.1 | async-start | bytes 4194304 | tf_op jit(solution)/shard_map/all_to_all | solution.py:120
  23.0 0.7 copy-start.2
  64.6 52.5 %all-to-all-start = ((bf16[16,128,512]{2,1,0:T(8,128)(2,1)}), bf16[16,128,512]{2,1,0:T(8,128)(2,1)}, u32[]{:S(2)}, u32[]{:S(2)}) async-start(bf16[16,128,512]{2,1,0:T(8,128)(2,1)} %copy.138), calls=%async_computation | async-start | bytes 4194304 | tf_op jit(solution)/shard_map/all_to_all | solution.py:119
  73.5 10.5 %copy-start.8 = (s32[32,8]{0,1:T(8,128)S(1)}, s32[32,8]{0,1:T(8,128)}, u32[]{:S(2)}) copy-start(s32[32,8]{0,1:T(8,128)} %param.18) | copy-start | bytes 3076
  73.5 93.0 %reduce-scatter.3.cloned.1.call-start = ((), (), s32[]{:S(2)}) async-start(), calls=%async_computation.6 | async-start | bytes 1572864 | tf_op jit(solution)/shard_map/reduce_scatter | solution.py:132
  75.2 24.9 %collective-permute-start = (bf16[128,512]{1,0:T(8,128)(2,1)}, bf16[128,512]{1,0:T(8,128)(2,1)}, u32[]{:S(2)}, u32[]{:S(2)}) collective-permute-start(bf16[128,512]{1,0:T(8,128)(2,1)} %get-tuple-element.7), channel_id=1, source_target_pairs={{0,2},{2,4},{4,6},{6,8},{8,10},{10,12},{12,14},{14,16},{16,18},{18... | collective-permute-start | bytes 393224 | tf_op jit(solution)/shard_map/ppermute | solution.py:14
  78.0 25.3 %collective-permute-start.1 = (bf16[128,512]{1,0:T(8,128)(2,1)}, bf16[128,512]{1,0:T(8,128)(2,1)}, u32[]{:S(2)}, u32[]{:S(2)}) collective-permute-start(bf16[128,512]{1,0:T(8,128)(2,1)} %get-tuple-element.5), channel_id=1, source_target_pairs={{0,2},{2,4},{4,6},{6,8},{8,10},{10,12},{12,14},{14,16},{16,18},{18... | collective-permute-start | bytes 393224 | tf_op jit(solution)/shard_map/ppermute | solution.py:14
  120.6 2.0 copy-start.6
  123.8 1.4 copy-start.1
  125.2 0.7 copy-start.9
  125.2 1.0 copy-start.3
  125.2 1.2 copy-start.4
  127.0 1.7 copy-start.7
  127.0 39.5 %copy-start.5 = (bf16[256,1024]{1,0:T(8,128)(2,1)S(1)}, bf16[256,1024]{1,0:T(8,128)(2,1)}, u32[]{:S(2)}) copy-start(bf16[256,1024]{1,0:T(8,128)(2,1)} %param.12) | copy-start | bytes 1572868
  128.7 46.1 %copy-start.10 = (f32[512]{0:T(512)S(1)}, f32[512]{0:T(512)}, u32[]{:S(2)}) copy-start(f32[512]{0:T(512)} %param.20) | copy-start | bytes 6148
  168.7 13.3 %all-to-all-start.2 = ((bf16[2,128,512]{2,0,1:T(2,128)(2,1)}), bf16[2,128,512]{2,0,1:T(2,128)(2,1)S(1)}, u32[]{:S(2)}, u32[]{:S(2)}) async-start(bf16[2,128,512]{2,0,1:T(2,128)(2,1)} %copy.155), calls=%async_computation.3 | async-start | bytes 524288 | tf_op jit(solution)/shard_map/all_to_all | solution.py:152
  174.7 58.3 %reduce-scatter.5.cloned.1.call-start = ((), (), s32[]{:S(2)}) async-start(), calls=%async_computation.7 | async-start | bytes 1572864 | tf_op jit(solution)/shard_map/reduce_scatter | solution.py:163
  196.3 9.6 %copy-start.12 = (f32[1024]{0:T(1024)S(1)}, f32[1024]{0:T(1024)}, u32[]{:S(2)}) copy-start(f32[1024]{0:T(1024)} %param.21) | copy-start | bytes 12292
Sparse Core Ops, SparseCore 0:
  128.8 37.6 reduce-scatter.2
  213.2 19.8 reduce-scatter.4
where the time goes:
time: 244 us; the launch traced here: 242 us
  waiting for transfers between devices  112 us (46%)
  local copies, waits for them, and re-layouts  33.6 us (14%)
  starting transfers between devices  26.6 us (11%)
  matrix products  25.2 us (10%)
  blocking collectives  22.1 us (9%)
  between operations  14 us (6%)
  other arithmetic  8.48 us (3%)
    reduce_scatter x1, waiting for transfers between devices, per_device(): lax.psum_scatter(jnp.dot(attended, output_weight, preferred_element_type=...  37.7 us
    all_to_all x1, waiting for transfers between devices, per_device(): lax.all_to_all(send_values, 'tm', split_axis=0, concat_axis=0, tiled=True)  37.6 us
    reduce_scatter x1, waiting for transfers between devices, per_device(): lax.psum_scatter(jnp.dot(hidden, down_weight, preferred_element_type=jnp....  20 us
    all_to_all x1, blocking collectives, per_device(): lax.all_to_all(states, 'tm', split_axis=0, concat_axis=1, tiled=True)  12.8 us
    all_gather x1, blocking collectives, per_device(): whole = lax.all_gather(second, 'mp', axis=1, tiled=True)  9.25 us
    all_to_all x1, starting transfers between devices, per_device(): lax.all_to_all(send_keys, 'tm', split_axis=0, concat_axis=0, tiled=True)  8.83 us
    all_to_all x1, waiting for transfers between devices, per_device(): lax.all_to_all(mixed, 'tm', split_axis=1, concat_axis=0, tiled=True)  7.23 us
    dot_general x1, matrix products, per_device(): jnp.dot(hidden, down_weight, preferred_element_type=jnp.float32)  7.13 us
  transfers between devices with their start and end apart: 7, of which 6 were waited for; matrix products, arithmetic and copies ran while one was open for 14% of the time, Pallas kernels for 0%

commit v1 on v0

v1 whole, which is shorter than its diff:
```python
import functools
import math

import jax
import jax.numpy as jnp
import numpy as np
from jax import lax
from jax.experimental import pallas as pl
from jax.experimental.pallas import tpu as pltpu
from jax.sharding import PartitionSpec as P

HD = 128
MESH = pl.DeviceIdType.MESH


def dot(a, b):
    return jnp.dot(a, b, preferred_element_type=jnp.float32)


def kernel(
    groups,
    parts,
    spans,
    rows,
    slot,
    tokens,
    gain1,
    pattern,
    decay,
    gain2,
    spread,
    degree,
    gather,
    wq,
    wk,
    wv,
    wo,
    wu,
    wd,
    out,
    qkv_w,
    out_w,
    up_w,
    down_w,
    normed,
    queries,
    kv,
    sel,
    tops,
    totals,
    acc,
    attended,
    proj_send,
    proj_recv,
    first,
    mix,
    got,
    smooth,
    back,
    second,
    hidden,
    ff_send,
    ff_recv,
    w_sem,
    far_s,
    far_r,
    proj_s,
    proj_r,
    mix_s,
    mix_r,
    back_s,
    back_r,
    sec_s,
    sec_r,
    ff_s,
    ff_r,
):
    g = lax.axis_index("tm")
    m = lax.axis_index("mp")
    sites = kv.shape[1]
    width = kv.shape[2] // 2
    heads = width // HD
    cols = out.shape[1]
    units = hidden.shape[1]

    loads = [
        pltpu.make_async_copy(wk, qkv_w.at[:, pl.ds(0, width)], w_sem.at[0]),
        pltpu.make_async_copy(wv, qkv_w.at[:, pl.ds(width, width)], w_sem.at[1]),
        pltpu.make_async_copy(wq, qkv_w.at[:, pl.ds(2 * width, width)], w_sem.at[2]),
        pltpu.make_async_copy(wo, out_w, w_sem.at[3]),
        pltpu.make_async_copy(wu, up_w, w_sem.at[4]),
        pltpu.make_async_copy(wd, down_w, w_sem.at[5]),
    ]
    for load in loads:
        load.start()

    barrier = pltpu.get_barrier_semaphore()

    def greet(step, carry):
        pl.semaphore_signal(
            barrier, inc=1, device_id=(lax.rem(g + step, groups), m), device_id_type=MESH
        )
        return carry

    lax.fori_loop(1, groups, greet, 0)
    for step in range(1, parts):
        pl.semaphore_signal(
            barrier, inc=1, device_id=(g, lax.rem(m + step, parts)), device_id_type=MESH
        )

    wide = tokens[...].astype(jnp.float32)
    square = jnp.mean(wide * wide, axis=-1, keepdims=True)
    normed[...] = (wide * lax.rsqrt(square + 1e-05) * gain1[...]).astype(jnp.bfloat16)

    for j in range(2):
        loads[j].wait()
        product = dot(normed[...], qkv_w[:, pl.ds(j * width, width)]).astype(jnp.bfloat16)
        kv[0, :, pl.ds(j * width, width)] = product[:sites]
        kv[1, :, pl.ds(j * width, width)] = product[sites:]
    for i, span in enumerate(spans[1:]):
        target = jnp.minimum(g + span, groups - 1)
        pick = lax.rem(jnp.maximum(pattern[2 * target, 3 + i], 0), 2).astype(jnp.float32)
        sel[i] = (
            kv[0].astype(jnp.float32) * (1.0 - pick) + kv[1].astype(jnp.float32) * pick
        ).astype(jnp.bfloat16)

    pl.semaphore_wait(barrier, groups + parts - 2)

    def far_copy(i):
        source = kv.at[pl.ds(0, 2)] if i == 0 else sel.at[pl.ds(i - 1, 1)]
        target = kv.at[pl.ds(2, 2)] if i == 0 else kv.at[pl.ds(3 + i, 1)]
        return pltpu.make_async_remote_copy(
            src_ref=source,
            dst_ref=target,
            send_sem=far_s.at[i],
            recv_sem=far_r.at[i],
            device_id=(jnp.minimum(g + spans[i], groups - 1), m),
            device_id_type=MESH,
        )

    for i in reversed(range(len(spans))):

        @pl.when(g + spans[i] < groups)
        def _(i=i):
            far_copy(i).start()

    loads[2].wait()
    queries[...] = dot(normed[...], qkv_w[:, pl.ds(2 * width, width)]).astype(jnp.bfloat16)

    scale = 1.0 / math.sqrt(HD)

    def attend(start, count, hide, fresh):
        for h in range(heads):
            at = pl.ds(h * HD, HD)
            keys = kv[pl.ds(start, count), :, at].reshape(count * sites, HD)
            values = kv[pl.ds(start, count), :, pl.ds(width + h * HD, HD)].reshape(
                count * sites, HD
            )
            scores = (
                lax.dot_general(
                    queries[:, at],
                    keys,
                    (((1,), (1,)), ((), ())),
                    preferred_element_type=jnp.float32,
                )
                * scale
            )
            if hide is not None:
                step = lax.broadcasted_iota(jnp.int32, scores.shape, 0) // sites
                block = lax.broadcasted_iota(jnp.int32, scores.shape, 1) // sites
                scores = jnp.where((step == hide[0]) & (block == hide[1]), -jnp.inf, scores)
            top = jnp.max(scores, axis=-1, keepdims=True)
            if fresh:
                probs = jnp.exp(scores - top)
                total = jnp.sum(probs, axis=-1, keepdims=True)
                part = dot(probs.astype(jnp.bfloat16), values)
            else:
                old = tops[h][:, :1]
                top = jnp.maximum(top, old)
                factor = jnp.exp(old - top)
                probs = jnp.exp(scores - top)
                total = totals[h][:, :1] * factor + jnp.sum(probs, axis=-1, keepdims=True)
                part = acc[:, at] * factor + dot(probs.astype(jnp.bfloat16), values)
            tops[h] = jnp.broadcast_to(top, tops.shape[1:])
            totals[h] = jnp.broadcast_to(total, totals.shape[1:])
            acc[:, at] = part

    attend(0, 2, (0, 1), True)
    for i, span in enumerate(spans):

        @pl.when(g >= span)
        def _(i=i):
            far_copy(i).wait_recv()
            if i == 0:
                attend(2, 2, (1, 1), False)
            else:
                attend(3 + i, 1, None, False)

    for h in range(heads):
        at = pl.ds(h * HD, HD)
        attended[:, at] = (acc[:, at] / totals[h][:, :1]).astype(jnp.bfloat16)

    own = pl.ds(pl.multiple_of(m * cols, cols), cols)

    def peer_of(step):
        return lax.rem(m + step, parts)

    def peer_columns(step):
        return pl.ds(pl.multiple_of(peer_of(step) * cols, cols), cols)

    def proj_copy(step):
        return pltpu.make_async_remote_copy(
            src_ref=proj_send.at[step - 1],
            dst_ref=proj_recv.at[step - 1],
            send_sem=proj_s.at[step - 1],
            recv_sem=proj_r.at[step - 1],
            device_id=(g, peer_of(step)),
            device_id_type=MESH,
        )

    loads[3].wait()
    for step in range(1, parts):
        proj_send[step - 1] = dot(attended[...], out_w[:, peer_columns(step)]).astype(jnp.bfloat16)
        proj_copy(step).start()
    summed = tokens[:, own].astype(jnp.float32) + dot(attended[...], out_w[:, own])
    for step in range(1, parts):
        proj_copy(step).wait_recv()
        summed = summed + proj_recv[step - 1].astype(jnp.float32)
    first[...] = summed.astype(jnp.bfloat16)

    mix[...] = (dot(spread[...], first[...]) / degree[...]).astype(jnp.bfloat16)

    def share(index):
        return pl.ds(pl.multiple_of(index * rows, rows), rows)

    def mix_copy(step):
        peer = lax.rem(g + step, groups)
        return pltpu.make_async_remote_copy(
            src_ref=mix.at[share(peer)],
            dst_ref=got.at[share(g)],
            send_sem=mix_s.at[step],
            recv_sem=mix_r.at[step],
            device_id=(peer, m),
            device_id_type=MESH,
        )

    def mix_start(step, carry):
        mix_copy(step).start()
        return carry

    lax.fori_loop(1, groups, mix_start, 0)
    got[share(g)] = mix[share(g)]

    def back_copy(step):
        peer = lax.rem(g + step, groups)
        return pltpu.make_async_remote_copy(
            src_ref=smooth.at[share(peer)],
            dst_ref=back.at[share(g)],
            send_sem=back_s.at[step],
            recv_sem=back_r.at[step],
            device_id=(peer, m),
            device_id_type=MESH,
        )

    retain = jnp.exp(-decay[...])
    inject = jnp.sqrt(1.0 - retain * retain)

    def advance(index, state):
        @pl.when(index != g)
        def _():
            step = lax.rem(g - index + groups, groups)
            pltpu.make_async_remote_copy(
                src_ref=mix.at[share(index)],
                dst_ref=got.at[share(index)],
                send_sem=mix_s.at[step],
                recv_sem=mix_r.at[step],
                device_id=(index, m),
                device_id_type=MESH,
            ).wait_recv()

        frames = got[share(index)].astype(jnp.float32)
        early = retain * state + inject * frames[:slot]
        late = retain * early + inject * frames[slot:]
        smooth[share(index)] = jnp.concatenate([early, late], axis=0).astype(jnp.bfloat16)

        @pl.when(index != g)
        def _():
            back_copy(lax.rem(index - g + groups, groups)).start()

        return late

    lax.fori_loop(0, groups, advance, jnp.zeros((slot, cols), jnp.float32))
    back[share(g)] = smooth[share(g)]

    def back_wait(step, carry):
        source = lax.rem(g - step + groups, groups)
        pltpu.make_async_remote_copy(
            src_ref=smooth.at[share(source)],
            dst_ref=back.at[share(source)],
            send_sem=back_s.at[step],
            recv_sem=back_r.at[step],
            device_id=(source, m),
            device_id_type=MESH,
        ).wait_recv()
        return carry

    lax.fori_loop(1, groups, back_wait, 0)

    second[m] = (first[...].astype(jnp.float32) + dot(gather[...], back[...])).astype(jnp.bfloat16)

    def second_copy(step, slot_of):
        return pltpu.make_async_remote_copy(
            src_ref=second.at[m],
            dst_ref=second.at[slot_of],
            send_sem=sec_s.at[step - 1],
            recv_sem=sec_r.at[step - 1],
            device_id=(g, peer_of(step)),
            device_id_type=MESH,
        )

    for step in range(1, parts):
        second_copy(step, m).start()
    for step in range(1, parts):
        second_copy(step, lax.rem(m - step + parts, parts)).wait_recv()

    square = 0.0
    for j in range(parts):
        wide = second[j].astype(jnp.float32)
        square = square + jnp.sum(wide * wide, axis=-1, keepdims=True)
    factor = lax.rsqrt(square * (1.0 / (parts * cols)) + 1e-05)
    for j in range(parts):
        at = pl.ds(j * cols, cols)
        normed[:, at] = (second[j].astype(jnp.float32) * factor * gain2[:, at]).astype(jnp.bfloat16)

    tile = min(512, units)
    loads[4].wait()

    def expand(index, carry):
        at = pl.ds(pl.multiple_of(index * tile, tile), tile)
        hidden[:, at] = jax.nn.gelu(dot(normed[...], up_w[:, at]), approximate=True).astype(
            jnp.bfloat16
        )
        return carry

    lax.fori_loop(0, units // tile, expand, 0)

    def ff_copy(step):
        return pltpu.make_async_remote_copy(
            src_ref=ff_send.at[step - 1],
            dst_ref=ff_recv.at[step - 1],
            send_sem=ff_s.at[step - 1],
            recv_sem=ff_r.at[step - 1],
            device_id=(g, peer_of(step)),
            device_id_type=MESH,
        )

    loads[5].wait()
    for step in range(1, parts):
        ff_send[step - 1] = dot(hidden[...], down_w[:, peer_columns(step)]).astype(jnp.bfloat16)
        ff_copy(step).start()
    summed = second[m].astype(jnp.float32) + dot(hidden[...], down_w[:, own])
    for step in range(1, parts):
        ff_copy(step).wait_recv()
        summed = summed + ff_recv[step - 1].astype(jnp.float32)
    out[...] = summed.astype(jnp.bfloat16)

    for i, span in enumerate(spans):

        @pl.when(g + span < groups)
        def _(i=i):
            far_copy(i).wait_send()

    for step in range(1, parts):
        proj_copy(step).wait_send()
        second_copy(step, m).wait_send()
        ff_copy(step).wait_send()

    def drain(step, carry):
        mix_copy(step).wait_send()
        back_copy(step).wait_send()
        return carry

    lax.fori_loop(1, groups, drain, 0)


def per_device(
    tokens,
    norm1_gain,
    query_weight,
    key_weight,
    value_weight,
    output_weight,
    pattern,
    adjacency,
    decay_rate,
    norm2_gain,
    up_weight,
    down_weight,
):
    groups = lax.axis_size("tm")
    parts = lax.axis_size("mp")
    count, features = tokens.shape
    width = query_weight.shape[1]
    sites = adjacency.shape[0]
    steps = count // sites
    assert steps == 2
    cols = features // parts
    units = up_weight.shape[1]
    spans = [1 << k for k in range(pattern.shape[1] - 2) if 1 << k < groups]
    far = len(spans) - 1
    each = sites // groups
    slot = max(8, each)
    rows = steps * slot
    bf16, f32 = jnp.bfloat16, jnp.float32

    links = jnp.maximum(adjacency, jnp.eye(sites, dtype=jnp.int32))
    degree = jnp.sum(links, axis=1).astype(f32)
    lines = jnp.pad(links.reshape(groups, each, sites), ((0, 0), (0, slot - each), (0, 0)))
    step_eye = np.eye(steps, dtype=np.int32)[None, :, None, :, None]
    spread = (
        (lines[:, None, :, None, :] * step_eye).reshape(groups * rows, steps * sites).astype(bf16)
    )
    degree = jnp.pad(degree.reshape(groups, 1, each), ((0, 0), (0, 0), (0, slot - each)), constant_values=1.0)
    degree = jnp.broadcast_to(degree, (groups, steps, slot)).reshape(groups * rows, 1)
    place = np.zeros((steps, sites, groups, steps, slot), np.float32)
    for site in range(sites):
        for step in range(steps):
            place[step, site, site // each, step, site % each] = 1.0
    gather = jnp.asarray(place.reshape(count, groups * rows), bf16)

    vmem = pl.BlockSpec(memory_space=pltpu.VMEM)
    smem = pl.BlockSpec(memory_space=pltpu.SMEM)
    hbm = pl.BlockSpec(memory_space=pl.ANY)
    others = max(1, parts - 1)
    dma = pltpu.SemaphoreType.DMA
    return pl.pallas_call(
        functools.partial(kernel, groups, parts, spans, rows, slot),
        out_shape=jax.ShapeDtypeStruct((count, cols), bf16),
        in_specs=[vmem, vmem, smem] + [vmem] * 5 + [hbm] * 6,
        out_specs=vmem,
        scratch_shapes=[
            pltpu.VMEM((features, 3 * width), bf16),
            pltpu.VMEM((width, features), bf16),
            pltpu.VMEM((features, units), bf16),
            pltpu.VMEM((units, features), bf16),
            pltpu.VMEM((count, features), bf16),
            pltpu.VMEM((count, width), bf16),
            pltpu.VMEM((4 + far, sites, 2 * width), bf16),
            pltpu.VMEM((max(1, far), sites, 2 * width), bf16),
            pltpu.VMEM((width // HD, count, HD), f32),
            pltpu.VMEM((width // HD, count, HD), f32),
            pltpu.VMEM((count, width), f32),
            pltpu.VMEM((count, width), bf16),
            pltpu.VMEM((others, count, cols), bf16),
            pltpu.VMEM((others, count, cols), bf16),
            pltpu.VMEM((count, cols), bf16),
            pltpu.VMEM((groups * rows, cols), bf16),
            pltpu.VMEM((groups * rows, cols), bf16),
            pltpu.VMEM((groups * rows, cols), bf16),
            pltpu.VMEM((groups * rows, cols), bf16),
            pltpu.VMEM((parts, count, cols), bf16),
            pltpu.VMEM((count, units), bf16),
            pltpu.VMEM((others, count, cols), bf16),
            pltpu.VMEM((others, count, cols), bf16),
            dma((6,)),
            dma((len(spans),)),
            dma((len(spans),)),
            dma((others,)),
            dma((others,)),
            dma((groups,)),
            dma((groups,)),
            dma((groups,)),
            dma((groups,)),
            dma((others,)),
            dma((others,)),
            dma((others,)),
            dma((others,)),
        ],
        compiler_params=pltpu.CompilerParams(
            collective_id=0, has_side_effects=True, vmem_limit_bytes=48 * 1024 * 1024
        ),
    )(
        tokens,
        norm1_gain.reshape(1, -1),
        pattern,
        decay_rate.reshape(1, -1),
        norm2_gain.reshape(1, -1),
        spread,
        degree,
        gather,
        query_weight,
        key_weight,
        value_weight,
        output_weight,
        up_weight,
        down_weight,
    )


def solution(mesh):
    placed = (
        P("tm", None),
        P(),
        P(None, "mp"),
        P(None, "mp"),
        P(None, "mp"),
        P("mp", None),
        P(),
        P(),
        P("mp"),
        P(),
        P(None, "mp"),
        P("mp", None),
    )
    return jax.shard_map(
        per_device, mesh=mesh, in_specs=placed, out_specs=P("tm", "mp"), check_vma=False
    )
```

time: 244 us -> 96.6 us (0.40)
  waiting for transfers between devices: 112 us -> 0 us
  Pallas kernels: 0 us -> 83.8 us
  starting transfers between devices: 26.6 us -> 0 us
  matrix products: 25.2 us -> 0 us
  local copies, waits for them, and re-layouts: 33.6 us -> 10.6 us
  blocking collectives: 22.1 us -> 0 us
  between operations: 14 us -> 0.06 us
  other arithmetic: 8.48 us -> 1.73 us
    pallas_call x0 -> x1, Pallas kernels: none -> 83.8 us  [per_device(): pl.pallas_call(functools.partial(kernel, groups, parts, spans, rows, slot...]
    reduce_scatter x2 -> x0, waiting for transfers between devices: 57.7 us -> none  [the longest x1 37.7 us: per_device(): lax.psum_scatter(jnp.dot(attended, output_weight, preferred_element_type=...]
    all_to_all x3 -> x0, waiting for transfers between devices: 49.2 us -> none  [the longest x1 37.6 us: per_device(): lax.all_to_all(send_values, 'tm', split_axis=0, concat_axis=0, tiled=True)]
    dot_general x14 -> x0, matrix products: 25.2 us -> none  [the longest x1 7.13 us: per_device(): jnp.dot(hidden, down_weight, preferred_element_type=jnp.float32)]
    all_to_all x3 -> x0, starting transfers between devices: 21 us -> none  [the longest x1 8.83 us: per_device(): lax.all_to_all(send_keys, 'tm', split_axis=0, concat_axis=0, tiled=True)]
    all_to_all x1 -> x0, blocking collectives: 12.8 us -> none  [per_device(): lax.all_to_all(states, 'tm', split_axis=0, concat_axis=1, tiled=True)]
    gather x4 -> x0, local copies, waits for them, and re-layouts: 9.87 us -> none  [the longest x2 5.39 us: per_device(): got_keys[source]]
    all_gather x1 -> x0, blocking collectives: 9.25 us -> none  [per_device(): whole = lax.all_gather(second, 'mp', axis=1, tiled=True)]
  transfers between devices with their start and end apart: 7 -> 0, of which waited for: 6 -> 0; matrix products, arithmetic and copies ran while one was open for 14% -> 0% of each run, Pallas kernels for 0% -> 0%
where the time goes in v1:
time: 96.6 us; the launch traced here: 96.1 us
  Pallas kernels  83.8 us (87%)
  local copies, waits for them, and re-layouts  10.6 us (11%)
  other arithmetic  1.73 us (2%)
    pallas_call x1, Pallas kernels, per_device(): pl.pallas_call(functools.partial(kernel, groups, parts, spans, rows, slot...  83.8 us
    unnamed x20, local copies, waits for them, and re-layouts  10.4 us

profile of v1, /device:TPU:24, one launch (start us, length us, event | category | flops | bytes accessed | tf_op | source)
XLA Modules:
  0.0 96.1 jit_solution(5221387805302699861)
XLA Ops:
  0.0 0.8 copy.16.pattern
  0.8 0.9 fusion
  1.7 0.1 convert_element_type.22
  1.8 0.1 reshape.31.degree
  1.9 0.8 multiply_convert_fusion
  2.7 0.0 copy-start
  2.7 1.2 %copy-done = bf16[1024,512]{1,0:T(8,128)(2,1)S(1)} copy-done((bf16[1024,512]{1,0:T(8,128)(2,1)S(1)}, bf16[1024,512]{1,0:T(8,128)(2,1)}, u32[]{:S(2)}) %copy-start) | copy-done | bytes 1048600
  4.0 0.0 copy-start.1
  4.0 1.2 %copy-done.1 = bf16[1024,512]{1,0:T(8,128)(2,1)S(1)} copy-done((bf16[1024,512]{1,0:T(8,128)(2,1)S(1)}, bf16[1024,512]{1,0:T(8,128)(2,1)}, u32[]{:S(2)}) %copy-start.1) | copy-done | bytes 1048600
  5.2 0.0 copy-start.2
  5.2 1.2 %copy-done.2 = bf16[1024,512]{1,0:T(8,128)(2,1)S(1)} copy-done((bf16[1024,512]{1,0:T(8,128)(2,1)S(1)}, bf16[1024,512]{1,0:T(8,128)(2,1)}, u32[]{:S(2)}) %copy-start.2) | copy-done | bytes 1048600
  6.4 0.0 copy-start.3
  6.4 1.2 %copy-done.3 = bf16[512,1024]{1,0:T(8,128)(2,1)S(1)} copy-done((bf16[512,1024]{1,0:T(8,128)(2,1)S(1)}, bf16[512,1024]{1,0:T(8,128)(2,1)}, u32[]{:S(2)}) %copy-start.3) | copy-done | bytes 1048600
  7.6 0.0 copy-start.4
  7.6 1.0 %copy-done.4 = bf16[256,1024]{1,0:T(8,128)(2,1)S(1)} copy-done((bf16[256,1024]{1,0:T(8,128)(2,1)S(1)}, bf16[256,1024]{1,0:T(8,128)(2,1)}, u32[]{:S(2)}) %copy-start.4) | copy-done | bytes 524312
  8.7 0.0 copy-start.5
  8.7 0.9 copy-done.5
  9.6 0.0 copy-start.6
  9.6 0.7 copy-done.6
  10.3 0.0 copy-start.7
  10.3 0.7 copy-done.7
  11.0 0.0 copy-start.8
  11.0 0.7 copy-done.8
  11.6 83.8 %shard_map.136 = bf16[256,512]{1,0:T(8,128)(2,1)S(1)} custom-call(bf16[256,1024]{1,0:T(8,128)(2,1)S(1)} %copy-done.4, f32[1,1024]{1,0:T(1,128)S(1)} %bitcast.7, s32[32,8]{1,0:T(8,128)S(1)} %copy.16.pattern, f32[1,512]{1,0:T(1,128)S(1)} %bitcast.9, f32[1,1024]{1,0:T(1,128)S(1)} %bitcast.8, bf16[256,256]{1,0:T(8,128)(2,1)S(1)} %bitcast.6, ...), custom_call_target="tpu_custom_call" | custom-call | tf_op jit(solution)/shard_map/pallas_call | solution.py:436
  95.4 0.7 copy.19
  (2 shorter events, 0.0 us)
Async XLA Ops:
  2.7 1.2 %copy-start = (bf16[1024,512]{1,0:T(8,128)(2,1)S(1)}, bf16[1024,512]{1,0:T(8,128)(2,1)}, u32[]{:S(2)}) copy-start(bf16[1024,512]{1,0:T(8,128)(2,1)} %wq.1) | copy-start | bytes 3145732
  4.0 1.2 %copy-start.1 = (bf16[1024,512]{1,0:T(8,128)(2,1)S(1)}, bf16[1024,512]{1,0:T(8,128)(2,1)}, u32[]{:S(2)}) copy-start(bf16[1024,512]{1,0:T(8,128)(2,1)} %wk.1) | copy-start | bytes 3145732
  5.2 1.2 %copy-start.2 = (bf16[1024,512]{1,0:T(8,128)(2,1)S(1)}, bf16[1024,512]{1,0:T(8,128)(2,1)}, u32[]{:S(2)}) copy-start(bf16[1024,512]{1,0:T(8,128)(2,1)} %wv.1) | copy-start | bytes 3145732
  6.4 1.2 %copy-start.3 = (bf16[512,1024]{1,0:T(8,128)(2,1)S(1)}, bf16[512,1024]{1,0:T(8,128)(2,1)}, u32[]{:S(2)}) copy-start(bf16[512,1024]{1,0:T(8,128)(2,1)} %wo.1) | copy-start | bytes 3145732
  7.6 1.0 %copy-start.4 = (bf16[256,1024]{1,0:T(8,128)(2,1)S(1)}, bf16[256,1024]{1,0:T(8,128)(2,1)}, u32[]{:S(2)}) copy-start(bf16[256,1024]{1,0:T(8,128)(2,1)} %tokens.1) | copy-start | bytes 1572868
  8.7 0.9 copy-start.5
  9.6 0.7 copy-start.6
  10.3 0.7 copy-start.7
  11.0 0.7 copy-start.8

commit v2 on v1

--- a/solution.py
+++ b/solution.py
@@ -3,7 +3,6 @@
 
 import jax
 import jax.numpy as jnp
-import numpy as np
 from jax import lax
 from jax.experimental import pallas as pl
 from jax.experimental.pallas import tpu as pltpu
@@ -23,14 +22,12 @@
     spans,
     rows,
     slot,
-    tokens,
-    gain1,
     pattern,
-    decay,
-    gain2,
-    spread,
-    degree,
-    gather,
+    tokens_in,
+    gain1_in,
+    gain2_in,
+    decay_in,
+    adjacency_in,
     wq,
     wk,
     wv,
@@ -38,6 +35,13 @@
     wu,
     wd,
     out,
+    tokens,
+    gain1,
+    gain2,
+    decay,
+    adjacency,
+    spread,
+    gather,
     qkv_w,
     out_w,
     up_w,
@@ -61,6 +65,7 @@
     hidden,
     ff_send,
     ff_recv,
+    in_sem,
     w_sem,
     far_s,
     far_r,
@@ -83,6 +88,15 @@
     cols = out.shape[1]
     units = hidden.shape[1]
 
+    inputs = [
+        pltpu.make_async_copy(tokens_in, tokens, in_sem.at[0]),
+        pltpu.make_async_copy(gain1_in, gain1, in_sem.at[1]),
+        pltpu.make_async_copy(gain2_in, gain2, in_sem.at[2]),
+        pltpu.make_async_copy(decay_in, decay, in_sem.at[3]),
+        pltpu.make_async_copy(adjacency_in, adjacency, in_sem.at[4]),
+    ]
+    for load in inputs:
+        load.start()
     loads = [
         pltpu.make_async_copy(wk, qkv_w.at[:, pl.ds(0, width)], w_sem.at[0]),
         pltpu.make_async_copy(wv, qkv_w.at[:, pl.ds(width, width)], w_sem.at[1]),
@@ -108,6 +122,8 @@
             barrier, inc=1, device_id=(g, lax.rem(m + step, parts)), device_id_type=MESH
         )
 
+    for load in inputs:
+        load.wait()
     wide = tokens[...].astype(jnp.float32)
     square = jnp.mean(wide * wide, axis=-1, keepdims=True)
     normed[...] = (wide * lax.rsqrt(square + 1e-05) * gain1[...]).astype(jnp.bfloat16)
@@ -119,7 +135,7 @@
         kv[1, :, pl.ds(j * width, width)] = product[sites:]
     for i, span in enumerate(spans[1:]):
         target = jnp.minimum(g + span, groups - 1)
-        pick = lax.rem(jnp.maximum(pattern[2 * target, 3 + i], 0), 2).astype(jnp.float32)
+        pick = lax.rem(jnp.maximum(pattern[3 + i, 2 * target], 0), 2).astype(jnp.float32)
         sel[i] = (
             kv[0].astype(jnp.float32) * (1.0 - pick) + kv[1].astype(jnp.float32) * pick
         ).astype(jnp.bfloat16)
@@ -146,6 +162,29 @@
 
     loads[2].wait()
     queries[...] = dot(normed[...], qkv_w[:, pl.ds(2 * width, width)]).astype(jnp.bfloat16)
+
+    each = sites // groups
+    line = lax.broadcasted_iota(jnp.int32, adjacency.shape, 0)
+    other = lax.broadcasted_iota(jnp.int32, adjacency.shape, 1)
+    links = jnp.where(line == other, 1, adjacency[...]).astype(jnp.float32).astype(jnp.bfloat16)
+    for step in range(2):
+        packed = lax.broadcasted_iota(jnp.int32, (groups * rows, sites), 0)
+        site = lax.broadcasted_iota(jnp.int32, (groups * rows, sites), 1)
+        inner = packed % rows
+        spot = inner % slot
+        here = (inner // slot == step) & (spot < each) & (packed // rows * each + spot == site)
+        spread[:, pl.ds(step * sites, sites)] = dot(
+            jnp.where(here, 1.0, 0.0).astype(jnp.bfloat16), links
+        ).astype(jnp.bfloat16)
+        site = lax.broadcasted_iota(jnp.int32, (sites, groups * rows), 0)
+        packed = lax.broadcasted_iota(jnp.int32, (sites, groups * rows), 1)
+        inner = packed % rows
+        spot = inner % slot
+        here = (inner // slot == step) & (spot < each) & (packed // rows * each + spot == site)
+        gather[pl.ds(step * sites, sites), :] = jnp.where(here, 1.0, 0.0).astype(jnp.bfloat16)
+    degree = jnp.maximum(
+        jnp.sum(spread[...].astype(jnp.float32), axis=-1, keepdims=True), 1.0
+    )
 
     scale = 1.0 / math.sqrt(HD)
 
@@ -228,7 +267,7 @@
         summed = summed + proj_recv[step - 1].astype(jnp.float32)
     first[...] = summed.astype(jnp.bfloat16)
 
-    mix[...] = (dot(spread[...], first[...]) / degree[...]).astype(jnp.bfloat16)
+    mix[...] = (dot(spread[...], first[...]) / degree).astype(jnp.bfloat16)
 
     def share(index):
         return pl.ds(pl.multiple_of(index * rows, rows), rows)
@@ -413,21 +452,6 @@
     rows = steps * slot
     bf16, f32 = jnp.bfloat16, jnp.float32
 
-    links = jnp.maximum(adjacency, jnp.eye(sites, dtype=jnp.int32))
-    degree = jnp.sum(links, axis=1).astype(f32)
-    lines = jnp.pad(links.reshape(groups, each, sites), ((0, 0), (0, slot - each), (0, 0)))
-    step_eye = np.eye(steps, dtype=np.int32)[None, :, None, :, None]
-    spread = (
-        (lines[:, None, :, None, :] * step_eye).reshape(groups * rows, steps * sites).astype(bf16)
-    )
-    degree = jnp.pad(degree.reshape(groups, 1, each), ((0, 0), (0, 0), (0, slot - each)), constant_values=1.0)
-    degree = jnp.broadcast_to(degree, (groups, steps, slot)).reshape(groups * rows, 1)
-    place = np.zeros((steps, sites, groups, steps, slot), np.float32)
-    for site in range(sites):
-        for step in range(steps):
-            place[step, site, site // each, step, site % each] = 1.0
-    gather = jnp.asarray(place.reshape(count, groups * rows), bf16)
-
     vmem = pl.BlockSpec(memory_space=pltpu.VMEM)
     smem = pl.BlockSpec(memory_space=pltpu.SMEM)
     hbm = pl.BlockSpec(memory_space=pl.ANY)
@@ -436,9 +460,16 @@
     return pl.pallas_call(
         functools.partial(kernel, groups, parts, spans, rows, slot),
         out_shape=jax.ShapeDtypeStruct((count, cols), bf16),
-        in_specs=[vmem, vmem, smem] + [vmem] * 5 + [hbm] * 6,
+        in_specs=[smem] + [hbm] * 11,
         out_specs=vmem,
         scratch_shapes=[
+            pltpu.VMEM((count, features), bf16),
+            pltpu.VMEM((1, features), f32),
+            pltpu.VMEM((1, features), f32),
+            pltpu.VMEM((1, cols), f32),
+            pltpu.VMEM((sites, sites), jnp.int32),
+            pltpu.VMEM((groups * rows, count), bf16),
+            pltpu.VMEM((count, groups * rows), bf16),
             pltpu.VMEM((features, 3 * width), bf16),
             pltpu.VMEM((width, features), bf16),
             pltpu.VMEM((features, units), bf16),
@@ -462,6 +493,7 @@
             pltpu.VMEM((count, units), bf16),
             pltpu.VMEM((others, count, cols), bf16),
             pltpu.VMEM((others, count, cols), bf16),
+            dma((5,)),
             dma((6,)),
             dma((len(spans),)),
             dma((len(spans),)),
@@ -477,17 +509,15 @@
             dma((others,)),
         ],
         compiler_params=pltpu.CompilerParams(
-            collective_id=0, has_side_effects=True, vmem_limit_bytes=48 * 1024 * 1024
+            collective_id=0, has_side_effects=True, vmem_limit_bytes=60 * 1024 * 1024
         ),
     )(
+        pattern.T,
         tokens,
         norm1_gain.reshape(1, -1),
-        pattern,
+        norm2_gain.reshape(1, -1),
         decay_rate.reshape(1, -1),
-        norm2_gain.reshape(1, -1),
-        spread,
-        degree,
-        gather,
+        adjacency,
         query_weight,
         key_weight,
         value_weight,

time: 96.6 us -> 87.8 us (0.909)
  local copies, waits for them, and re-layouts: 10.6 us -> 1.67 us
  Pallas kernels: 83.8 us -> 85.9 us
  other arithmetic: 1.73 us -> 0 us
    unnamed x20 -> x1, local copies, waits for them, and re-layouts: 10.4 us -> 1.67 us
    pallas_call x1, Pallas kernels: 83.8 us -> 85.9 us  [per_device(): pl.pallas_call(functools.partial(kernel, groups, parts, spans, rows, slot...]
where the time goes in v2:
time: 87.8 us; the launch traced here: 87.6 us
  Pallas kernels  85.9 us (98%)
  local copies, waits for them, and re-layouts  1.67 us (2%)
    pallas_call x1, Pallas kernels, per_device(): pl.pallas_call(functools.partial(kernel, groups, parts, spans, rows, slot...  85.9 us

profile of v2, /device:TPU:24, one launch (start us, length us, event | category | flops | bytes accessed | tf_op | source)
XLA Modules:
  0.0 87.6 jit_solution(9361821403266040423)
XLA Ops:
  0.0 85.9 %shard_map.118 = bf16[256,512]{1,0:T(8,128)(2,1)} custom-call(s32[8,32]{1,0:T(8,128)} %bitcast.4, bf16[256,1024]{1,0:T(8,128)(2,1)} %tokens_in.1, f32[1,1024]{1,0:T(1,128)} %bitcast.5, f32[1,1024]{1,0:T(1,128)} %bitcast.6, f32[1,512]{1,0:T(1,128)} %bitcast.7, s32[128,128]{1,0:T(8,128)} %adjacency_in.1, bf16[1024,512]{1,0:T(8,128)(2,1)} %wq.1, ...), custom_call_target="tpu_custom_call" | custom-call | tf_op jit(solution)/shard_map/pallas_call | solution.py:460
  85.9 1.7 %copy.14 = bf16[256,512]{1,0:T(8,128)(2,1)} copy(bf16[256,512]{1,0:T(8,128)(2,1)} %shard_map.118) | data formatting | bytes 524288

commit v3 on v2

--- a/solution.py
+++ b/solution.py
@@ -49,6 +49,8 @@
     normed,
     queries,
     kv,
+    shared,
+    far,
     sel,
     tops,
     totals,
@@ -69,6 +71,8 @@
     w_sem,
     far_s,
     far_r,
+    pass_s,
+    pass_r,
     proj_s,
     proj_r,
     mix_s,
@@ -124,6 +128,49 @@
 
     for load in inputs:
         load.wait()
+    own = pl.ds(pl.multiple_of(m * cols, cols), cols)
+    shared[...] = tokens[:, own]
+    for i, span in enumerate(spans[1:]):
+        target = jnp.minimum(g + span, groups - 1)
+        pick = lax.rem(jnp.maximum(pattern[3 + i, 2 * target], 0), 2).astype(jnp.float32)
+        sel[i] = (
+            shared[:sites].astype(jnp.float32) * (1.0 - pick)
+            + shared[sites:].astype(jnp.float32) * pick
+        ).astype(jnp.bfloat16)
+
+    def peer_of(step):
+        return lax.rem(m + step, parts)
+
+    def far_rows(i):
+        return pl.ds(0, 2 * sites) if i == 0 else pl.ds((1 + i) * sites, sites)
+
+    def far_copy(i):
+        return pltpu.make_async_remote_copy(
+            src_ref=shared if i == 0 else sel.at[i - 1],
+            dst_ref=far.at[m, far_rows(i)],
+            send_sem=far_s.at[i],
+            recv_sem=far_r.at[i],
+            device_id=(jnp.minimum(g + spans[i], groups - 1), m),
+            device_id_type=MESH,
+        )
+
+    def pass_copy(i, step, part):
+        return pltpu.make_async_remote_copy(
+            src_ref=far.at[m, far_rows(i)],
+            dst_ref=far.at[part, far_rows(i)],
+            send_sem=pass_s.at[i, step - 1],
+            recv_sem=pass_r.at[i, step - 1],
+            device_id=(g, peer_of(step)),
+            device_id_type=MESH,
+        )
+
+    pl.semaphore_wait(barrier, groups + parts - 2)
+    for i in reversed(range(len(spans))):
+
+        @pl.when(g + spans[i] < groups)
+        def _(i=i):
+            far_copy(i).start()
+
     wide = tokens[...].astype(jnp.float32)
     square = jnp.mean(wide * wide, axis=-1, keepdims=True)
     normed[...] = (wide * lax.rsqrt(square + 1e-05) * gain1[...]).astype(jnp.bfloat16)
@@ -133,33 +180,6 @@
         product = dot(normed[...], qkv_w[:, pl.ds(j * width, width)]).astype(jnp.bfloat16)
         kv[0, :, pl.ds(j * width, width)] = product[:sites]
         kv[1, :, pl.ds(j * width, width)] = product[sites:]
-    for i, span in enumerate(spans[1:]):
-        target = jnp.minimum(g + span, groups - 1)
-        pick = lax.rem(jnp.maximum(pattern[3 + i, 2 * target], 0), 2).astype(jnp.float32)
-        sel[i] = (
-            kv[0].astype(jnp.float32) * (1.0 - pick) + kv[1].astype(jnp.float32) * pick
-        ).astype(jnp.bfloat16)
-
-    pl.semaphore_wait(barrier, groups + parts - 2)
-
-    def far_copy(i):
-        source = kv.at[pl.ds(0, 2)] if i == 0 else sel.at[pl.ds(i - 1, 1)]
-        target = kv.at[pl.ds(2, 2)] if i == 0 else kv.at[pl.ds(3 + i, 1)]
-        return pltpu.make_async_remote_copy(
-            src_ref=source,
-            dst_ref=target,
-            send_sem=far_s.at[i],
-            recv_sem=far_r.at[i],
-            device_id=(jnp.minimum(g + spans[i], groups - 1), m),
-            device_id_type=MESH,
-        )
-
-    for i in reversed(range(len(spans))):
-
-        @pl.when(g + spans[i] < groups)
-        def _(i=i):
-            far_copy(i).start()
-
     loads[2].wait()
     queries[...] = dot(normed[...], qkv_w[:, pl.ds(2 * width, width)]).astype(jnp.bfloat16)
 
@@ -224,25 +244,50 @@
             totals[h] = jnp.broadcast_to(total, totals.shape[1:])
             acc[:, at] = part
 
+    def hand_on(i):
+        @pl.when(g >= spans[i])
+        def _():
+            far_copy(i).wait_recv()
+            for step in range(1, parts):
+                pass_copy(i, step, m).start()
+
+    def absorb(i):
+        at_rows = far_rows(i)
+        blocks = 2 if i == 0 else 1
+        start = 2 if i == 0 else 3 + i
+
+        @pl.when(g >= spans[i])
+        def _():
+            for step in range(1, parts):
+                pass_copy(i, step, lax.rem(m - step + parts, parts)).wait_recv()
+            square = 0.0
+            for j in range(parts):
+                wide = far[j, at_rows].astype(jnp.float32)
+                square = square + jnp.sum(wide * wide, axis=-1, keepdims=True)
+            factor = lax.rsqrt(square * (1.0 / (parts * cols)) + 1e-05)
+            count = blocks * sites
+            for j in range(parts):
+                at = pl.ds(j * cols, cols)
+                normed[pl.ds(0, count), at] = (
+                    far[j, at_rows].astype(jnp.float32) * factor * gain1[:, at]
+                ).astype(jnp.bfloat16)
+            for j in range(2):
+                at = pl.ds(j * width, width)
+                product = dot(normed[pl.ds(0, count), :], qkv_w[:, at]).astype(jnp.bfloat16)
+                for block in range(blocks):
+                    kv[start + block, :, at] = product[block * sites : (block + 1) * sites]
+            attend(start, blocks, (1, 1) if i == 0 else None, False)
+
+    hand_on(0)
     attend(0, 2, (0, 1), True)
-    for i, span in enumerate(spans):
-
-        @pl.when(g >= span)
-        def _(i=i):
-            far_copy(i).wait_recv()
-            if i == 0:
-                attend(2, 2, (1, 1), False)
-            else:
-                attend(3 + i, 1, None, False)
+    for i in range(1, len(spans)):
+        hand_on(i)
+        absorb(i - 1)
+    absorb(len(spans) - 1)
 
     for h in range(heads):
         at = pl.ds(h * HD, HD)
         attended[:, at] = (acc[:, at] / totals[h][:, :1]).astype(jnp.bfloat16)
-
-    own = pl.ds(pl.multiple_of(m * cols, cols), cols)
-
-    def peer_of(step):
-        return lax.rem(m + step, parts)
 
     def peer_columns(step):
         return pl.ds(pl.multiple_of(peer_of(step) * cols, cols), cols)
@@ -261,7 +306,7 @@
     for step in range(1, parts):
         proj_send[step - 1] = dot(attended[...], out_w[:, peer_columns(step)]).astype(jnp.bfloat16)
         proj_copy(step).start()
-    summed = tokens[:, own].astype(jnp.float32) + dot(attended[...], out_w[:, own])
+    summed = shared[...].astype(jnp.float32) + dot(attended[...], out_w[:, own])
     for step in range(1, parts):
         proj_copy(step).wait_recv()
         summed = summed + proj_recv[step - 1].astype(jnp.float32)
@@ -408,6 +453,11 @@
         @pl.when(g + span < groups)
         def _(i=i):
             far_copy(i).wait_send()
+
+        @pl.when(g >= span)
+        def _(i=i):
+            for step in range(1, parts):
+                pass_copy(i, step, m).wait_send()
 
     for step in range(1, parts):
         proj_copy(step).wait_send()
@@ -477,7 +527,9 @@
             pltpu.VMEM((count, features), bf16),
             pltpu.VMEM((count, width), bf16),
             pltpu.VMEM((4 + far, sites, 2 * width), bf16),
-            pltpu.VMEM((max(1, far), sites, 2 * width), bf16),
+            pltpu.VMEM((count, cols), bf16),
+            pltpu.VMEM((parts, (2 + far) * sites, cols), bf16),
+            pltpu.VMEM((max(1, far), sites, cols), bf16),
             pltpu.VMEM((width // HD, count, HD), f32),
             pltpu.VMEM((width // HD, count, HD), f32),
             pltpu.VMEM((count, width), f32),
@@ -497,6 +549,8 @@
             dma((6,)),
             dma((len(spans),)),
             dma((len(spans),)),
+            dma((len(spans), others)),
+            dma((len(spans), others)),
             dma((others,)),
             dma((others,)),
             dma((groups,)),

time: 87.8 us -> 84.6 us (0.964)
  Pallas kernels: 85.9 us -> 82.7 us
    pallas_call x1, Pallas kernels: 85.9 us -> 82.7 us  [per_device(): pl.pallas_call(functools.partial(kernel, groups, parts, spans, rows, slot...]
where the time goes in v3:
time: 84.6 us; the launch traced here: 84.4 us
  Pallas kernels  82.7 us (98%)
  local copies, waits for them, and re-layouts  1.67 us (2%)
    pallas_call x1, Pallas kernels, per_device(): pl.pallas_call(functools.partial(kernel, groups, parts, spans, rows, slot...  82.7 us

profile of v3, /device:TPU:24, one launch (start us, length us, event | category | flops | bytes accessed | tf_op | source)
XLA Modules:
  0.0 84.4 jit_solution(4333837382766014412)
XLA Ops:
  0.0 82.7 %shard_map.118 = bf16[256,512]{1,0:T(8,128)(2,1)} custom-call(s32[8,32]{1,0:T(8,128)} %bitcast.4, bf16[256,1024]{1,0:T(8,128)(2,1)} %tokens_in.1, f32[1,1024]{1,0:T(1,128)} %bitcast.5, f32[1,1024]{1,0:T(1,128)} %bitcast.6, f32[1,512]{1,0:T(1,128)} %bitcast.7, s32[128,128]{1,0:T(8,128)} %adjacency_in.1, bf16[1024,512]{1,0:T(8,128)(2,1)} %wq.1, ...), custom_call_target="tpu_custom_call" | custom-call | tf_op jit(solution)/shard_map/pallas_call | solution.py:510
  82.8 1.7 %copy.14 = bf16[256,512]{1,0:T(8,128)(2,1)} copy(bf16[256,512]{1,0:T(8,128)(2,1)} %shard_map.118) | data formatting | bytes 524288

commit v4 on v3

--- a/solution.py
+++ b/solution.py
@@ -165,7 +165,7 @@
         )
 
     pl.semaphore_wait(barrier, groups + parts - 2)
-    for i in reversed(range(len(spans))):
+    for i in range(len(spans)):
 
         @pl.when(g + spans[i] < groups)
         def _(i=i):

time: 84.6 us -> 73.9 us (0.87)
  Pallas kernels: 82.7 us -> 72 us
    pallas_call x1, Pallas kernels: 82.7 us -> 72 us  [per_device(): pl.pallas_call(functools.partial(kernel, groups, parts, spans, rows, slot...]
where the time goes in v4:
time: 73.9 us; the launch traced here: 73.7 us
  Pallas kernels  72 us (97%)
  local copies, waits for them, and re-layouts  1.67 us (2%)
    pallas_call x1, Pallas kernels, per_device(): pl.pallas_call(functools.partial(kernel, groups, parts, spans, rows, slot...  72 us
    unnamed x1, local copies, waits for them, and re-layouts  1.67 us

profile of v4, /device:TPU:24, one launch (start us, length us, event | category | flops | bytes accessed | tf_op | source)
XLA Modules:
  0.0 73.7 jit_solution(14476648420235299263)
XLA Ops:
  0.0 72.0 %shard_map.118 = bf16[256,512]{1,0:T(8,128)(2,1)} custom-call(s32[8,32]{1,0:T(8,128)} %bitcast.4, bf16[256,1024]{1,0:T(8,128)(2,1)} %tokens_in.1, f32[1,1024]{1,0:T(1,128)} %bitcast.5, f32[1,1024]{1,0:T(1,128)} %bitcast.6, f32[1,512]{1,0:T(1,128)} %bitcast.7, s32[128,128]{1,0:T(8,128)} %adjacency_in.1, bf16[1024,512]{1,0:T(8,128)(2,1)} %wq.1, ...), custom_call_target="tpu_custom_call" | custom-call | tf_op jit(solution)/shard_map/pallas_call | solution.py:510
  72.0 1.7 %copy.14 = bf16[256,512]{1,0:T(8,128)(2,1)} copy(bf16[256,512]{1,0:T(8,128)(2,1)} %shard_map.118) | data formatting | bytes 524288
